TPU v7x, 32 devices: a whole 2x2x4 slice. The times are simulated.
32 devices in a mesh: row: 16 (over z, y, core), col: 2 (over x).
Axes of the slice: x: 2, y: 2, z: 4, core: 2. Of those that a mesh axis runs over, the one named last changes fastest.
Arguments:
- slab: bfloat16 [16384, 4096], P('row', 'col'), may hold values from -6 to 6
- panel_left: bfloat16 [16384, 512], P('row', 'col'), may hold values from -3 to 3
- panel_top: bfloat16 [512, 4096], P('row', 'col'), may hold values from -3 to 3
- row_bases: bfloat16 [16384, 256], P('row'), may hold values from -0.25 to 0.25
- col_bases: bfloat16 [4096, 256], P('col'), may hold values from -0.25 to 0.25
- row_ranks: int32 [32], P('row'), may hold values from 32 to 256, as said below
- col_ranks: int32 [8], P('col'), may hold values from 32 to 256, as said below
- pivot_inverse: bfloat16 [512, 512], replicated, may hold values from -0.0625 to 0.0625
- pivot_rhs: bfloat16 [512, 1024], P('row', 'col'), may hold values from -6 to 6
- rhs: bfloat16 [16384, 1024], P('row', 'col'), may hold values from -6 to 6
Outputs:
- slab_new: bfloat16 [16384, 4096], P('row', 'col')
- rhs_new: bfloat16 [16384, 1024], P('row', 'col')
Inputs may be any that keep to these rules, and one draw needn't show every extreme that they name: `row_ranks`: each entry is the rank of one tile; the value 256 occurs in every draw. `col_ranks`: each entry is the rank of one tile; the value 256 occurs in every draw.
All inputs are finite; a program needn't handle non-finite values.
Results may differ from a plain program's by a relative error of at most 0.0062.
Values may be sent and summed in bfloat16 or wider, within the bound.
A program may use at most 128 MiB of HBM per device.

v0:
```python
import jax
import jax.numpy as jnp
from jax import lax
from jax.sharding import PartitionSpec as P


def per_device(
    slab,
    panel_left,
    panel_top,
    row_bases,
    col_bases,
    row_ranks,
    col_ranks,
    pivot_inverse,
    pivot_rhs,
    rhs,
):
    tile_order = pivot_inverse.shape[0]
    rank_width = row_bases.shape[1]
    row_count = row_ranks.shape[0]
    column_count = col_ranks.shape[0]
    gain_width = rhs.shape[1]
    levels = jnp.arange(rank_width, dtype=jnp.int32)
    keep_row = (levels[None, :] < row_ranks[:, None]).astype(jnp.float32)
    keep_column = (levels[None, :] < col_ranks[:, None]).astype(jnp.float32)
    left_bases = row_bases.reshape(row_count, tile_order, rank_width)
    right_bases = col_bases.reshape(column_count, tile_order, rank_width)
    left_tiles = panel_left.reshape(row_count, tile_order, panel_left.shape[1])
    part_core = jnp.einsum(
        "tbr,tbc->trc", left_bases, left_tiles, preferred_element_type=jnp.float32
    )
    part_core = (part_core * keep_row[:, :, None]).astype(jnp.bfloat16)
    row_core = lax.all_gather(part_core, "col", axis=2, tiled=True)
    shaped = panel_top.reshape(panel_top.shape[0], column_count, tile_order)
    projected = jnp.einsum("pjc,jcr->pjr", shaped, right_bases, preferred_element_type=jnp.float32)
    column_core = lax.all_gather(
        (projected * keep_column[None]).astype(jnp.bfloat16), "row", axis=0, tiled=True
    )
    solved = jnp.dot(
        pivot_inverse,
        lax.all_gather(pivot_rhs, "row", axis=0, tiled=True),
        preferred_element_type=jnp.float32,
    )
    core_block = jnp.einsum(
        "irp,pjs->ijrs", row_core, column_core, preferred_element_type=jnp.float32
    ).astype(jnp.bfloat16)
    spread = jnp.einsum(
        "ibr,ijrs->ijbs", left_bases, core_block, preferred_element_type=jnp.float32
    ).astype(jnp.bfloat16)
    change = jnp.einsum("ijbs,jcs->ibjc", spread, right_bases, preferred_element_type=jnp.float32)
    change = change.reshape(row_count * tile_order, column_count * tile_order)
    slab_new = (slab.astype(jnp.float32) - change).astype(jnp.bfloat16)
    pivot_solution = solved.astype(jnp.bfloat16)
    reduced = jnp.einsum(
        "irp,pg->irg", row_core, pivot_solution, preferred_element_type=jnp.float32
    ).astype(jnp.bfloat16)
    lowered = jnp.einsum("ibr,irg->ibg", left_bases, reduced, preferred_element_type=jnp.float32)
    lowered = lowered.reshape(row_count * tile_order, gain_width)
    rhs_new = (rhs.astype(jnp.float32) - lowered).astype(jnp.bfloat16)
    return (slab_new, rhs_new)


def solution(mesh):
    in_specs = (
        P("row", "col"),
        P("row", "col"),
        P("row", "col"),
        P("row", None),
        P("col", None),
        P("row"),
        P("col"),
        P(),
        P("row", "col"),
        P("row", "col"),
    )
    out_specs = (P("row", "col"), P("row", "col"))
    return jax.shard_map(
        per_device, mesh=mesh, in_specs=in_specs, out_specs=out_specs, check_vma=False
    )
```

profile of v0, /device:TPU:1, one launch (start us, length us, event | category | flops | bytes accessed | tf_op | source)
XLA Modules:
  0.0 90.4 jit_solution(14266718456039538815)
XLA Ops:
  7.2 0.0 copy-start
  7.2 0.0 copy-start.3
  7.2 0.0 all-gather.2.cloned.1.call-start
  7.2 0.8 fusion.15
  8.1 0.3 copy-done
  8.4 1.2 %fusion.10 = bf16[32,4,256]{2,0,1:T(8,128)(2,1)S(1)} fusion(bf16[4,512,256]{2,1,0:T(8,128)(2,1)S(1)} %bitcast.49, bf16[4,4,8,512]{3,2,1,0:T(8,128)(2,1)} %bitcast.56, f32[4,256]{1,0:T(4,128)S(1)} %fusion.15), kind=kOutput, calls=%fused_computation.17 | convolution fusion | flops 33619968 | bytes 1249280 | tf_op jit(solution)/shard_map/pjc,jcr->pjr/dot_general | solution.py:36
  9.6 0.7 copy.16
  10.3 0.0 all-gather.2.cloned.1.call-update
  10.3 0.7 compare_convert_fusion
  11.0 1.6 %fusion.8 = bf16[2,256,256]{2,1,0:T(8,128)(2,1)S(1)} fusion(bf16[2,512,256]{2,1,0:T(8,128)(2,1)} %bitcast.52, bf16[2,512,256]{2,1,0:T(8,128)(2,1)} %bitcast.55, f32[2,256]{1,0:T(2,128)S(1)} %compare_convert_fusion), kind=kOutput, calls=%fused_computation.14 | convolution fusion | flops 134479872 | bytes 1312768 | tf_op jit(solution)/shard_map/tbr,tbc->trc/dot_general | solution.py:30
  12.6 8.8 %all_gather.10 = bf16[2,256,512]{2,1,0:T(8,128)(2,1)} all-gather(bf16[2,256,256]{2,1,0:T(8,128)(2,1)S(1)} %fusion.8), channel_id=1, replica_groups=mesh['row'=16,'col'=2] {'col'}, dimensions={2}, use_global_device_ids=true | all-gather | bytes 786432 | tf_op jit(solution)/shard_map/all_gather | solution.py:34
  21.4 25.4 %all_gather.11 = bf16[512,512]{1,0:T(8,128)(2,1)S(1)} all-gather(bf16[32,512]{1,0:T(8,128)(2,1)} %param.18), channel_id=1, replica_groups=mesh['row'=16,'col'=2] {'row'}, dimensions={0}, use_global_device_ids=true | all-gather | bytes 557056 | tf_op jit(solution)/shard_map/all_gather | solution.py:42
  46.8 0.0 copy-done.3
  46.8 1.2 %fusion.6 = bf16[512,512,1]{1,0,2:T(8,128)(2,1)} fusion(bf16[512,512]{1,0:T(8,128)(2,1)S(1)} %copy-done.3, bf16[512,512]{1,0:T(8,128)(2,1)S(1)} %all_gather.11), kind=kOutput, calls=%fused_computation.12 | convolution fusion | flops 268697600 | bytes 1572864 | tf_op jit(solution)/shard_map/dot_general | solution.py:40
  48.0 2.1 %fusion.7 = f32[2,512,512]{1,2,0:T(8,128)S(1)} fusion(bf16[2,512,256]{2,1,0:T(8,128)(2,1)} %bitcast.53, bf16[2,256,512]{2,1,0:T(8,128)(2,1)} %all_gather.10, bf16[512,512,1]{1,0,2:T(8,128)(2,1)} %fusion.6), kind=kOutput, calls=%fused_computation.13 | convolution fusion | flops 537133056 | bytes 3670016 | tf_op jit(solution)/shard_map/ibr,irg->ibg/dot_general | solution.py:58
  50.2 2.7 %fusion = bf16[1024,512]{1,0:T(8,128)(2,1)} fusion(f32[2,512,512]{1,2,0:T(8,128)S(1)} %fusion.7, bf16[1024,512]{1,0:T(8,128)(2,1)} %param.19), kind=kLoop, calls=%fused_computation.3 | loop fusion | flops 1572864 | bytes 4194304 | tf_op jit(solution)/shard_map/convert_element_type | solution.py:60
  52.9 0.0 copy-start.1
  52.9 0.0 all-gather.2.cloned.1.call-done
  52.9 2.2 %fusion.5 = bf16[2,4,256,256]{2,3,0,1:T(8,128)(2,1)S(1)} fusion(bf16[512,4,256,1]{2,1,0,3:T(4,128)(2,1)} %bitcast.57, bf16[2,256,512]{2,1,0:T(8,128)(2,1)} %all_gather.10), kind=kOutput, calls=%fused_computation.8 | convolution fusion | flops 537395200 | bytes 2621440 | tf_op jit(solution)/shard_map/irp,pjs->ijrs/dot_general | solution.py:45
  55.1 0.0 copy-done.1
  55.1 5.1 %convolution_bitcast_fusion = f32[2,512,4,512]{3,1,0,2:T(8,128)} fusion(bf16[4,512,256,1]{2,1,3,0:T(8,128)(2,1)S(1)} %bitcast.48, bf16[2,4,256,256]{2,3,0,1:T(8,128)(2,1)S(1)} %fusion.5, bf16[2,512,256,1]{2,1,0,3:T(8,128)(2,1)S(1)} %bitcast.54), kind=kOutput, calls=%fused_computation.1 | convolution fusion | flops 1611661312 | bytes 11010048 | tf_op jit(solution)/shard_map/ijbs,jcs->ibjc/dot_general | solution.py:51
  60.1 12.0 %copy.20 = f32[2,512,4,512]{3,2,1,0:T(4,128)} copy(f32[2,512,4,512]{3,1,0,2:T(8,128)} %convolution_bitcast_fusion) | data formatting | bytes 16777216 | tf_op jit(solution)/shard_map/ijbs,jcs->ibjc/transpose | solution.py:51
  72.1 0.0 copy-start.2
  72.1 7.8 %copy.28 = f32[128,8,4,512]{3,1,2,0:T(8,128)S(1)} copy(f32[128,8,4,512]{3,2,1,0:T(4,128)} %bitcast.50) | data formatting | bytes 16777216
  80.0 0.0 copy-done.2
  80.0 3.5 %subtract_convert_fusion = bf16[1024,2048]{1,0:T(8,128)(2,1)} fusion(f32[1024,2048]{1,0:T(8,128)S(1)} %bitcast.51, bf16[1024,2048]{1,0:T(8,128)(2,1)S(1)} %copy-done.2), kind=kLoop, calls=%fused_computation | loop fusion | flops 6291456 | bytes 16777216 | tf_op jit(solution)/shard_map/convert_element_type | solution.py:53
Async XLA Ops:
  7.2 1.2 %copy-start = (bf16[2048,256]{1,0:T(8,128)(2,1)S(1)}, bf16[2048,256]{1,0:T(8,128)(2,1)}, u32[]{:S(2)}) copy-start(bf16[2048,256]{1,0:T(8,128)(2,1)} %param.14) | copy-start | bytes 3145732
  7.2 39.6 %copy-start.3 = (bf16[512,512]{1,0:T(8,128)(2,1)S(1)}, bf16[512,512]{1,0:T(8,128)(2,1)}, u32[]{:S(2)}) copy-start(bf16[512,512]{1,0:T(8,128)(2,1)} %param.17) | copy-start | bytes 1572868
  7.2 45.7 %all-gather.2.cloned.1.call-start = ((), (), s32[]{:S(2)}) async-start(), calls=%async_computation | async-start | bytes 1114112 | tf_op jit(solution)/shard_map/all_gather | solution.py:37
  52.9 2.2 %copy-start.1 = (bf16[1024,256]{1,0:T(8,128)(2,1)S(1)}, bf16[1024,256]{1,0:T(8,128)(2,1)}, u32[]{:S(2)}) copy-start(bf16[1024,256]{1,0:T(8,128)(2,1)} %param.13) | copy-start | bytes 1572868
  72.1 7.9 %copy-start.2 = (bf16[1024,2048]{1,0:T(8,128)(2,1)S(1)}, bf16[1024,2048]{1,0:T(8,128)(2,1)}, u32[]{:S(2)}) copy-start(bf16[1024,2048]{1,0:T(8,128)(2,1)} %param.10) | copy-start | bytes 12582916
Sparse Core Ops, SparseCore 0:
  10.8 40.8 all-gather.1
where the time goes:
time: 90.8 us; the launch traced here: 90.4 us
  blocking collectives  34.2 us (38%)
  local copies, waits for them, and re-layouts  20.9 us (23%)
  between operations  14.1 us (16%)
  matrix products  13.4 us (15%)
  other arithmetic  7.76 us (9%)
    all_gather x1, blocking collectives, per_device(): lax.all_gather(pivot_rhs, 'row', axis=0, tiled=True)  25.4 us
    transpose x1, local copies, waits for them, and re-layouts, per_device(): jnp.einsum('ijbs,jcs->ibjc', spread, right_bases, preferred_element_type=...  12 us
    all_gather x1, blocking collectives, per_device(): row_core = lax.all_gather(part_core, 'col', axis=2, tiled=True)  8.83 us
    unnamed x9, local copies, waits for them, and re-layouts  8.21 us
    dot_general x1, matrix products, per_device(): jnp.einsum('ijbs,jcs->ibjc', spread, right_bases, preferred_element_type=...  5.06 us
    convert_element_type x1, other arithmetic, per_device(): slab_new = (slab.astype(jnp.float32) - change).astype(jnp.bfloat16)  3.5 us
    convert_element_type x1, other arithmetic, per_device(): rhs_new = (rhs.astype(jnp.float32) - lowered).astype(jnp.bfloat16)  2.7 us
    dot_general x1, matrix products, per_device(): jnp.einsum('irp,pjs->ijrs', row_core, column_core, preferred_element_type...  2.17 us
  transfers between devices with their start and end apart: 1, of which 0 were waited for; matrix products, arithmetic and copies ran while one was open for 9% of the time, Pallas kernels for 0%

commit v1 on v0

v1 whole, which is shorter than its diff:
```python
import functools

import jax
import jax.numpy as jnp
from jax import lax
from jax.experimental import pallas as pl
from jax.experimental.pallas import tpu as pltpu
from jax.sharding import PartitionSpec as P

MESH = pl.DeviceIdType.MESH


def grid_of(count):
    cores = 2 if count % 2 == 0 else 1
    chips = count // cores
    inner = max(d for d in range(1, chips + 1) if chips % d == 0 and d * d <= chips)
    return chips // inner, inner, cores


def gather_kernel(
    n_row,
    n_col,
    col_ranks,
    row_ranks,
    top,
    right,
    left,
    bases,
    inverse,
    pivot,
    core_out,
    reduced_out,
    blocks,
    cores_k,
    block_send,
    block_recv,
    k_send,
    k_recv,
):
    outer, inner, cores = grid_of(n_row)
    order = inverse.shape[0]
    rank = bases.shape[1]
    n_tiles = row_ranks.shape[0]
    m_tiles = col_ranks.shape[0]
    width = left.shape[1]
    m_width = m_tiles * rank

    row = lax.axis_index("row")
    col = lax.axis_index("col")
    c = lax.rem(row, cores)
    b = lax.rem(row // cores, inner)
    a = row // (cores * inner)

    def index(a_, b_, c_):
        return (a_ * inner + b_) * cores + c_

    a_peers = [lax.rem(a + k, outer) for k in range(1, outer)]
    b_peers = [lax.rem(b + k, inner) for k in range(1, inner)]
    c_peers = [lax.rem(c + k, cores) for k in range(1, cores)]
    col_peers = [lax.rem(col + k, n_col) for k in range(1, n_col)]

    barrier = pltpu.get_barrier_semaphore()
    partners = [(index(p, b, c), col) for p in a_peers]
    partners += [(index(a, p, c), col) for p in b_peers]
    partners += [(index(a, b, p), col) for p in c_peers]
    partners += [(row, p) for p in col_peers]
    for partner in partners:
        pl.semaphore_signal(barrier, inc=1, device_id=partner, device_id_type=MESH)

    levels = lax.broadcasted_iota(jnp.int32, (1, rank), 1)
    for j in range(m_tiles):
        part = jnp.dot(
            top[:, j * order : (j + 1) * order],
            right[j * order : (j + 1) * order, :],
            preferred_element_type=jnp.float32,
        )
        part = jnp.where(levels < col_ranks[j], part, 0.0)
        blocks[row, :, j * rank : (j + 1) * rank] = part.astype(jnp.bfloat16)
    blocks[row, :, m_width:] = pivot[...]

    pl.semaphore_wait(barrier, len(partners))
    started = []

    def send(which, target):
        copy = pltpu.make_async_remote_copy(
            src_ref=blocks.at[which],
            dst_ref=blocks.at[which],
            send_sem=block_send.at[len(started)],
            recv_sem=block_recv.at[which],
            device_id=(target, col),
            device_id_type=MESH,
        )
        copy.start()
        started.append(copy)

    def arrived(which):
        pltpu.make_async_copy(blocks.at[which], blocks.at[which], block_recv.at[which]).wait()

    for p in reversed(a_peers):
        send(row, index(p, b, c))
    for p in b_peers:
        send(row, index(a, p, c))
    for p in c_peers:
        send(row, index(a, b, p))

    rows = lax.broadcasted_iota(jnp.int32, (rank, 1), 0)
    for i in range(n_tiles):
        part = lax.dot_general(
            bases[i * order : (i + 1) * order, :],
            left[i * order : (i + 1) * order, :],
            (((0,), (0,)), ((), ())),
            preferred_element_type=jnp.float32,
        )
        part = jnp.where(rows < row_ranks[i], part, 0.0)
        cores_k[col, i] = part.astype(jnp.bfloat16)
    k_copies = []
    for number, p in enumerate(col_peers):
        copy = pltpu.make_async_remote_copy(
            src_ref=cores_k.at[col],
            dst_ref=cores_k.at[col],
            send_sem=k_send.at[number],
            recv_sem=k_recv.at[col],
            device_id=(row, p),
            device_id_type=MESH,
        )
        copy.start()
        k_copies.append(copy)

    def from_inner(a_):
        for p in b_peers:
            s = index(a_, p, c)
            arrived(s)
            for q in c_peers:
                send(s, index(a, b, q))

    previous = a
    for p in a_peers:
        s = index(p, b, c)
        arrived(s)
        for q in b_peers:
            send(s, index(a, q, c))
        for q in c_peers:
            send(s, index(a, b, q))
        from_inner(previous)
        previous = p

    for p in col_peers:
        pltpu.make_async_copy(cores_k.at[p], cores_k.at[p], k_recv.at[p]).wait()
    solvers = []
    for i in range(n_tiles):
        total = jnp.zeros((rank, order), jnp.float32)
        for k in range(n_col):
            total += jnp.dot(
                cores_k[k, i],
                inverse[k * width : (k + 1) * width, :],
                preferred_element_type=jnp.float32,
            )
        solvers.append(total.astype(jnp.bfloat16))

    from_inner(previous)
    for q in c_peers:
        for p in [a] + a_peers:
            for r in [b] + b_peers:
                arrived(index(p, r, q))

    depth = blocks.shape[1]
    share = n_row // n_col
    wide = blocks.shape[2]
    for i in range(n_tiles):
        total = jnp.zeros((rank, m_width), jnp.float32)
        for k in range(n_col):
            piece = blocks[k * share : (k + 1) * share, :, :m_width]
            total += jnp.dot(
                cores_k[k, i],
                piece.reshape(share * depth, m_width),
                preferred_element_type=jnp.float32,
            )
        core_out[i] = total.astype(jnp.bfloat16)
        gains = blocks[:, :, m_width:].reshape(order, wide - m_width)
        reduced_out[i] = jnp.dot(
            solvers[i], gains, preferred_element_type=jnp.float32
        ).astype(jnp.bfloat16)

    for copy in started + k_copies:
        copy.wait_send()


def update_kernel(bases, core, reduced, right, slab, rhs, slab_out, rhs_out):
    rank = bases.shape[1]
    m_tiles = core.shape[2] // rank
    order = right.shape[0] // m_tiles
    basis = bases[...]
    for j in range(m_tiles):
        spread = jnp.dot(
            basis, core[0, :, j * rank : (j + 1) * rank], preferred_element_type=jnp.float32
        ).astype(jnp.bfloat16)
        change = lax.dot_general(
            spread,
            right[j * order : (j + 1) * order, :],
            (((1,), (1,)), ((), ())),
            preferred_element_type=jnp.float32,
        )
        at = slice(j * order, (j + 1) * order)
        slab_out[:, at] = (slab[:, at].astype(jnp.float32) - change).astype(jnp.bfloat16)
    lowered = jnp.dot(basis, reduced[0], preferred_element_type=jnp.float32)
    rhs_out[...] = (rhs[...].astype(jnp.float32) - lowered).astype(jnp.bfloat16)


def per_device(
    n_row,
    n_col,
    slab,
    panel_left,
    panel_top,
    row_bases,
    col_bases,
    row_ranks,
    col_ranks,
    pivot_inverse,
    pivot_rhs,
    rhs,
):
    order = pivot_inverse.shape[0]
    rank = row_bases.shape[1]
    n_tiles = row_ranks.shape[0]
    m_tiles = col_ranks.shape[0]
    gains = rhs.shape[1]
    width = panel_left.shape[1]
    outer, inner, cores = grid_of(n_row)
    sends = (outer - 1) + outer * (inner - 1) + outer * inner * (cores - 1)
    vmem = pl.BlockSpec(memory_space=pltpu.VMEM)
    smem = pl.BlockSpec(memory_space=pltpu.SMEM)
    core, reduced = pl.pallas_call(
        functools.partial(gather_kernel, n_row, n_col),
        out_shape=(
            jax.ShapeDtypeStruct((n_tiles, rank, m_tiles * rank), jnp.bfloat16),
            jax.ShapeDtypeStruct((n_tiles, rank, gains), jnp.bfloat16),
        ),
        in_specs=[smem, smem] + [vmem] * 6,
        out_specs=(vmem, vmem),
        scratch_shapes=[
            pltpu.VMEM((n_row, pivot_rhs.shape[0], m_tiles * rank + gains), jnp.bfloat16),
            pltpu.VMEM((n_col, n_tiles, rank, width), jnp.bfloat16),
            pltpu.SemaphoreType.DMA((sends,)),
            pltpu.SemaphoreType.DMA((n_row,)),
            pltpu.SemaphoreType.DMA((max(n_col - 1, 1),)),
            pltpu.SemaphoreType.DMA((n_col,)),
        ],
        compiler_params=pltpu.CompilerParams(
            collective_id=0, has_side_effects=True, vmem_limit_bytes=24 * 2**20
        ),
        name="gather",
    )(col_ranks, row_ranks, panel_top, col_bases, panel_left, row_bases, pivot_inverse, pivot_rhs)

    step = order // 2
    per_tile = order // step
    rows, columns = slab.shape
    return pl.pallas_call(
        update_kernel,
        grid=(rows // step,),
        out_shape=(
            jax.ShapeDtypeStruct(slab.shape, slab.dtype),
            jax.ShapeDtypeStruct(rhs.shape, rhs.dtype),
        ),
        in_specs=[
            pl.BlockSpec((step, rank), lambda r: (r, 0)),
            pl.BlockSpec((1, rank, m_tiles * rank), lambda r: (r // per_tile, 0, 0)),
            pl.BlockSpec((1, rank, gains), lambda r: (r // per_tile, 0, 0)),
            pl.BlockSpec((columns, rank), lambda r: (0, 0)),
            pl.BlockSpec((step, columns), lambda r: (r, 0)),
            pl.BlockSpec((step, gains), lambda r: (r, 0)),
        ],
        out_specs=(
            pl.BlockSpec((step, columns), lambda r: (r, 0)),
            pl.BlockSpec((step, gains), lambda r: (r, 0)),
        ),
        compiler_params=pltpu.CompilerParams(vmem_limit_bytes=32 * 2**20),
        name="update",
    )(row_bases, core, reduced, col_bases, slab, rhs)


def solution(mesh):
    in_specs = (
        P("row", "col"),
        P("row", "col"),
        P("row", "col"),
        P("row", None),
        P("col", None),
        P("row"),
        P("col"),
        P(),
        P("row", "col"),
        P("row", "col"),
    )
    out_specs = (P("row", "col"), P("row", "col"))
    return jax.shard_map(
        functools.partial(per_device, mesh.shape["row"], mesh.shape["col"]),
        mesh=mesh,
        in_specs=in_specs,
        out_specs=out_specs,
        check_vma=False,
    )
```

time: 90.8 us -> 41.9 us (0.46)
  blocking collectives: 34.2 us -> 0 us
  Pallas kernels: 0 us -> 27.7 us
  between operations: 14.1 us -> 0.67 us
  matrix products: 13.4 us -> 0 us
  local copies, waits for them, and re-layouts: 20.9 us -> 13 us
  other arithmetic: 7.76 us -> 0 us
    all_gather x2 -> x0, blocking collectives: 34.2 us -> none  [the longest x1 25.4 us: per_device(): lax.all_gather(pivot_rhs, 'row', axis=0, tiled=True)]
    pallas_call x0 -> x2, Pallas kernels: none -> 27.7 us  [the longest x1 22.4 us: per_device(): pl.pallas_call(functools.partial(gather_kernel, n_row, n_col), out_shape=...]
    dot_general x6 -> x0, matrix products: 13.4 us -> none  [the longest x1 5.06 us: per_device(): jnp.einsum('ijbs,jcs->ibjc', spread, right_bases, preferred_element_type=...]
    transpose x1 -> x0, local copies, waits for them, and re-layouts: 12 us -> none  [per_device(): jnp.einsum('ijbs,jcs->ibjc', spread, right_bases, preferred_element_type=...]
    convert_element_type x4 -> x0, other arithmetic: 7.76 us -> none  [the longest x1 3.5 us: per_device(): slab_new = (slab.astype(jnp.float32) - change).astype(jnp.bfloat16)]
    unnamed x9 -> x24, local copies, waits for them, and re-layouts: 8.21 us -> 13 us
  transfers between devices with their start and end apart: 1 -> 0, of which waited for: 0 -> 0; matrix products, arithmetic and copies ran while one was open for 9% -> 0% of each run, Pallas kernels for 0% -> 0%
where the time goes in v1:
time: 41.9 us; the launch traced here: 41.4 us
  Pallas kernels  27.7 us (66%)
  local copies, waits for them, and re-layouts  13 us (31%)
  between operations  0.67 us (2%)
    pallas_call x1, Pallas kernels, per_device(): pl.pallas_call(functools.partial(gather_kernel, n_row, n_col), out_shape=...  22.4 us
    unnamed x24, local copies, waits for them, and re-layouts  13 us
    pallas_call x1, Pallas kernels, per_device(): pl.pallas_call(update_kernel, grid=(rows // step,), out_shape=(jax.ShapeD...  5.34 us

profile of v1, /device:TPU:1, one launch (start us, length us, event | category | flops | bytes accessed | tf_op | source)
XLA Modules:
  0.0 41.4 jit_solution(5606492273713212492)
XLA Ops:
  0.6 0.0 copy-start.1
  0.6 1.2 %copy-done.1 = bf16[2048,256]{1,0:T(8,128)(2,1)S(1)} copy-done((bf16[2048,256]{1,0:T(8,128)(2,1)S(1)}, bf16[2048,256]{1,0:T(8,128)(2,1)}, u32[]{:S(2)}) %copy-start.1) | copy-done | bytes 1048600
  1.9 0.0 copy-start.3
  1.9 1.0 %copy-done.3 = bf16[1024,256]{1,0:T(8,128)(2,1)S(1)} copy-done((bf16[1024,256]{1,0:T(8,128)(2,1)S(1)}, bf16[1024,256]{1,0:T(8,128)(2,1)}, u32[]{:S(2)}) %copy-start.3) | copy-done | bytes 524312
  2.9 0.0 copy-start.6
  2.9 1.0 %copy-done.6 = bf16[1024,256]{1,0:T(8,128)(2,1)S(1)} copy-done((bf16[1024,256]{1,0:T(8,128)(2,1)S(1)}, bf16[1024,256]{1,0:T(8,128)(2,1)}, u32[]{:S(2)}) %copy-start.6) | copy-done | bytes 524312
  3.9 0.0 copy-start.7
  3.9 1.0 %copy-done.7 = bf16[512,512]{1,0:T(8,128)(2,1)S(1)} copy-done((bf16[512,512]{1,0:T(8,128)(2,1)S(1)}, bf16[512,512]{1,0:T(8,128)(2,1)}, u32[]{:S(2)}) %copy-start.7) | copy-done | bytes 524312
  5.0 0.0 copy-start.8
  5.0 0.9 %copy-done.8 = bf16[32,2048]{1,0:T(8,128)(2,1)S(1)} copy-done((bf16[32,2048]{1,0:T(8,128)(2,1)S(1)}, bf16[32,2048]{1,0:T(8,128)(2,1)}, u32[]{:S(2)}) %copy-start.8) | copy-done | bytes 131096
  5.9 0.0 copy-start.9
  5.9 0.8 %copy-done.9 = bf16[32,512]{1,0:T(8,128)(2,1)S(1)} copy-done((bf16[32,512]{1,0:T(8,128)(2,1)S(1)}, bf16[32,512]{1,0:T(8,128)(2,1)}, u32[]{:S(2)}) %copy-start.9) | copy-done | bytes 32792
  6.6 0.0 copy-start.10
  6.7 0.7 %copy-done.10 = s32[4]{0:T(128)S(1)} copy-done((s32[4]{0:T(128)S(1)}, s32[4]{0:T(128)}, u32[]{:S(2)}) %copy-start.10) | copy-done | bytes 40
  7.3 0.0 copy-start.11
  7.3 0.7 %copy-done.11 = s32[2]{0:T(128)S(1)} copy-done((s32[2]{0:T(128)S(1)}, s32[2]{0:T(128)}, u32[]{:S(2)}) %copy-start.11) | copy-done | bytes 32
  8.0 22.4 %gather.1 = (bf16[2,256,1024]{2,1,0:T(8,128)(2,1)S(1)}, bf16[2,256,512]{2,1,0:T(8,128)(2,1)S(1)}) custom-call(s32[4]{0:T(128)S(1)} %copy-done.10, s32[2]{0:T(128)S(1)} %copy-done.11, bf16[32,2048]{1,0:T(8,128)(2,1)S(1)} %copy-done.8, bf16[2048,256]{1,0:T(8,128)(2,1)S(1)} %copy-done.1, bf16[1024,256]{1,0:T(8,128)(2,1)S(1)} %copy-done.6, ...), custom_call_target="tpu_custom_call" | custom-call | tf_op jit(solution)/shard_map/gather/pallas_call | solution.py:233
  30.3 0.0 copy-start
  30.3 2.2 %copy-done = bf16[1024,2048]{1,0:T(8,128)(2,1)S(1)} copy-done((bf16[1024,2048]{1,0:T(8,128)(2,1)S(1)}, bf16[1024,2048]{1,0:T(8,128)(2,1)}, u32[]{:S(2)}) %copy-start) | copy-done | bytes 4194328
  32.5 0.0 copy-start.2
  32.5 1.2 %copy-done.2 = bf16[2048,256]{1,0:T(8,128)(2,1)S(1)} copy-done((bf16[2048,256]{1,0:T(8,128)(2,1)S(1)}, bf16[2048,256]{1,0:T(8,128)(2,1)}, u32[]{:S(2)}) %copy-start.2) | copy-done | bytes 1048600
  33.7 0.0 copy-start.4
  33.7 1.0 %copy-done.4 = bf16[1024,256]{1,0:T(8,128)(2,1)S(1)} copy-done((bf16[1024,256]{1,0:T(8,128)(2,1)S(1)}, bf16[1024,256]{1,0:T(8,128)(2,1)}, u32[]{:S(2)}) %copy-start.4) | copy-done | bytes 524312
  34.8 0.0 copy-start.5
  34.8 1.2 %copy-done.5 = bf16[1024,512]{1,0:T(8,128)(2,1)S(1)} copy-done((bf16[1024,512]{1,0:T(8,128)(2,1)S(1)}, bf16[1024,512]{1,0:T(8,128)(2,1)}, u32[]{:S(2)}) %copy-start.5) | copy-done | bytes 1048600
  36.0 5.3 %update.1 = (bf16[1024,2048]{1,0:T(8,128)(2,1)}, bf16[1024,512]{1,0:T(8,128)(2,1)}) custom-call(bf16[1024,256]{1,0:T(8,128)(2,1)S(1)} %copy-done.4, bf16[2,256,1024]{2,1,0:T(8,128)(2,1)S(1)} %get-tuple-element.4.core, bf16[2,256,512]{2,1,0:T(8,128)(2,1)S(1)} %get-tuple-element.5.reduced, bf16[2048,256]{1,0:T(8,128)(2,1)S(1)} %copy-done.2, ...), custom_call_target="tpu_custom_call" | custom-call | tf_op jit(solution)/shard_map/update/pallas_call | solution.py:258
Async XLA Ops:
  0.6 1.2 %copy-start.1 = (bf16[2048,256]{1,0:T(8,128)(2,1)S(1)}, bf16[2048,256]{1,0:T(8,128)(2,1)}, u32[]{:S(2)}) copy-start(bf16[2048,256]{1,0:T(8,128)(2,1)} %right.3) | copy-start | bytes 3145732
  1.9 1.0 %copy-start.3 = (bf16[1024,256]{1,0:T(8,128)(2,1)S(1)}, bf16[1024,256]{1,0:T(8,128)(2,1)}, u32[]{:S(2)}) copy-start(bf16[1024,256]{1,0:T(8,128)(2,1)} %bases.3) | copy-start | bytes 1572868
  2.9 1.0 %copy-start.6 = (bf16[1024,256]{1,0:T(8,128)(2,1)S(1)}, bf16[1024,256]{1,0:T(8,128)(2,1)}, u32[]{:S(2)}) copy-start(bf16[1024,256]{1,0:T(8,128)(2,1)} %left.1) | copy-start | bytes 1572868
  3.9 1.0 %copy-start.7 = (bf16[512,512]{1,0:T(8,128)(2,1)S(1)}, bf16[512,512]{1,0:T(8,128)(2,1)}, u32[]{:S(2)}) copy-start(bf16[512,512]{1,0:T(8,128)(2,1)} %inverse.1) | copy-start | bytes 1572868
  5.0 0.9 %copy-start.8 = (bf16[32,2048]{1,0:T(8,128)(2,1)S(1)}, bf16[32,2048]{1,0:T(8,128)(2,1)}, u32[]{:S(2)}) copy-start(bf16[32,2048]{1,0:T(8,128)(2,1)} %top.1) | copy-start | bytes 393220
  5.9 0.8 %copy-start.9 = (bf16[32,512]{1,0:T(8,128)(2,1)S(1)}, bf16[32,512]{1,0:T(8,128)(2,1)}, u32[]{:S(2)}) copy-start(bf16[32,512]{1,0:T(8,128)(2,1)} %pivot.1) | copy-start | bytes 98308
  6.6 0.7 %copy-start.10 = (s32[4]{0:T(128)S(1)}, s32[4]{0:T(128)}, u32[]{:S(2)}) copy-start(s32[4]{0:T(128)} %col_ranks.1) | copy-start | bytes 52
  7.3 0.7 %copy-start.11 = (s32[2]{0:T(128)S(1)}, s32[2]{0:T(128)}, u32[]{:S(2)}) copy-start(s32[2]{0:T(128)} %row_ranks.1) | copy-start | bytes 28
  30.3 2.2 %copy-start = (bf16[1024,2048]{1,0:T(8,128)(2,1)S(1)}, bf16[1024,2048]{1,0:T(8,128)(2,1)}, u32[]{:S(2)}) copy-start(bf16[1024,2048]{1,0:T(8,128)(2,1)} %slab.1) | copy-start | bytes 12582916
  32.5 1.2 %copy-start.2 = (bf16[2048,256]{1,0:T(8,128)(2,1)S(1)}, bf16[2048,256]{1,0:T(8,128)(2,1)}, u32[]{:S(2)}) copy-start(bf16[2048,256]{1,0:T(8,128)(2,1)} %right.3) | copy-start | bytes 3145732
  33.7 1.0 %copy-start.4 = (bf16[1024,256]{1,0:T(8,128)(2,1)S(1)}, bf16[1024,256]{1,0:T(8,128)(2,1)}, u32[]{:S(2)}) copy-start(bf16[1024,256]{1,0:T(8,128)(2,1)} %bases.3) | copy-start | bytes 1572868
  34.8 1.2 %copy-start.5 = (bf16[1024,512]{1,0:T(8,128)(2,1)S(1)}, bf16[1024,512]{1,0:T(8,128)(2,1)}, u32[]{:S(2)}) copy-start(bf16[1024,512]{1,0:T(8,128)(2,1)} %rhs.1) | copy-start | bytes 3145732

commit v2 on v1

v2 whole, which is shorter than its diff:
```python
import functools

import jax
import jax.numpy as jnp
from jax import lax
from jax.experimental import pallas as pl
from jax.experimental.pallas import tpu as pltpu
from jax.sharding import PartitionSpec as P

MESH = pl.DeviceIdType.MESH


def grid_of(count):
    cores = 2 if count % 2 == 0 else 1
    chips = count // cores
    inner = max(d for d in range(1, chips + 1) if chips % d == 0 and d * d <= chips)
    return chips // inner, inner, cores


def gather_kernel(
    n_row,
    n_col,
    col_ranks_hbm,
    row_ranks_hbm,
    top_hbm,
    right_hbm,
    left_hbm,
    bases_hbm,
    inverse_hbm,
    pivot_hbm,
    core_out,
    reduced_out,
    col_ranks,
    row_ranks,
    top,
    right,
    left,
    bases,
    inverse,
    m_blocks,
    g_blocks,
    cores_k,
    load_sem,
    m_send,
    m_recv,
    g_send,
    g_recv,
    k_send,
    k_recv,
):
    outer, inner, cores = grid_of(n_row)
    order = inverse.shape[0]
    rank = bases.shape[1]
    n_tiles = row_ranks.shape[0]
    m_tiles = col_ranks.shape[0]
    width = left.shape[1]

    row = lax.axis_index("row")
    col = lax.axis_index("col")
    c = lax.rem(row, cores)
    b = lax.rem(row // cores, inner)
    a = row // (cores * inner)

    def index(a_, b_, c_):
        return (a_ * inner + b_) * cores + c_

    a_peers = [lax.rem(a + k, outer) for k in range(1, outer)]
    b_peers = [lax.rem(b + k, inner) for k in range(1, inner)]
    c_peers = [lax.rem(c + k, cores) for k in range(1, cores)]
    col_peers = [lax.rem(col + k, n_col) for k in range(1, n_col)]

    barrier = pltpu.get_barrier_semaphore()
    partners = [(index(p, b, c), col) for p in a_peers]
    partners += [(index(a, p, c), col) for p in b_peers]
    partners += [(index(a, b, p), col) for p in c_peers]
    partners += [(row, p) for p in col_peers]
    for partner in partners:
        pl.semaphore_signal(barrier, inc=1, device_id=partner, device_id_type=MESH)

    pairs = [
        (pivot_hbm, g_blocks.at[row]),
        (top_hbm, top),
        (right_hbm, right),
        (col_ranks_hbm, col_ranks),
        (row_ranks_hbm, row_ranks),
        (bases_hbm, bases),
        (left_hbm, left),
        (inverse_hbm, inverse),
    ]
    loads = [
        pltpu.make_async_copy(source, target, load_sem.at[number])
        for number, (source, target) in enumerate(pairs)
    ]
    for load in loads:
        load.start()

    def sender(blocks, send_sems, recv_sems):
        started = []

        def send(which, target):
            copy = pltpu.make_async_remote_copy(
                src_ref=blocks.at[which],
                dst_ref=blocks.at[which],
                send_sem=send_sems.at[len(started)],
                recv_sem=recv_sems.at[which],
                device_id=(target, col),
                device_id_type=MESH,
            )
            copy.start()
            started.append(copy)

        def arrived(which):
            pltpu.make_async_copy(blocks.at[which], blocks.at[which], recv_sems.at[which]).wait()

        return started, send, arrived

    g_started, g_move, g_arrived = sender(g_blocks, g_send, g_recv)
    m_started, m_move, m_arrived = sender(m_blocks, m_send, m_recv)

    def send_own(move):
        for p in reversed(a_peers):
            move(row, index(p, b, c))
        for p in b_peers:
            move(row, index(a, p, c))
        for p in c_peers:
            move(row, index(a, b, p))

    def from_outer(p, move, landed):
        s = index(p, b, c)
        landed(s)
        for q in b_peers:
            move(s, index(a, q, c))
        for q in c_peers:
            move(s, index(a, b, q))

    def from_inner(a_, move, landed):
        for p in b_peers:
            s = index(a_, p, c)
            landed(s)
            for q in c_peers:
                move(s, index(a, b, q))

    def from_cores(landed):
        for q in c_peers:
            for p in [a] + a_peers:
                for r in [b] + b_peers:
                    landed(index(p, r, q))

    loads[0].wait()
    pl.semaphore_wait(barrier, len(partners))
    send_own(g_move)

    for load in loads[1:5]:
        load.wait()
    levels = lax.broadcasted_iota(jnp.int32, (1, rank), 1)
    for j in range(m_tiles):
        part = jnp.dot(
            top[:, j * order : (j + 1) * order],
            right[j * order : (j + 1) * order, :],
            preferred_element_type=jnp.float32,
        )
        part = jnp.where(levels < col_ranks[j], part, 0.0)
        m_blocks[row, :, j * rank : (j + 1) * rank] = part.astype(jnp.bfloat16)
    send_own(m_move)

    for p in a_peers:
        from_outer(p, g_move, g_arrived)

    for load in loads[5:]:
        load.wait()
    rows = lax.broadcasted_iota(jnp.int32, (rank, 1), 0)
    for i in range(n_tiles):
        part = lax.dot_general(
            bases[i * order : (i + 1) * order, :],
            left[i * order : (i + 1) * order, :],
            (((0,), (0,)), ((), ())),
            preferred_element_type=jnp.float32,
        )
        part = jnp.where(rows < row_ranks[i], part, 0.0)
        cores_k[col, i] = part.astype(jnp.bfloat16)
    k_copies = []
    for number, p in enumerate(col_peers):
        copy = pltpu.make_async_remote_copy(
            src_ref=cores_k.at[col],
            dst_ref=cores_k.at[col],
            send_sem=k_send.at[number],
            recv_sem=k_recv.at[col],
            device_id=(row, p),
            device_id_type=MESH,
        )
        copy.start()
        k_copies.append(copy)

    previous = a
    for p in a_peers:
        from_inner(previous, g_move, g_arrived)
        from_outer(p, m_move, m_arrived)
        from_inner(previous, m_move, m_arrived)
        previous = p
    from_inner(previous, g_move, g_arrived)
    from_inner(previous, m_move, m_arrived)

    from_cores(g_arrived)
    solved = jnp.dot(
        inverse[...],
        g_blocks[...].reshape(order, g_blocks.shape[2]),
        preferred_element_type=jnp.float32,
    ).astype(jnp.bfloat16)
    for p in col_peers:
        pltpu.make_async_copy(cores_k.at[p], cores_k.at[p], k_recv.at[p]).wait()
    for i in range(n_tiles):
        total = jnp.zeros((rank, solved.shape[1]), jnp.float32)
        for k in range(n_col):
            total += jnp.dot(
                cores_k[k, i],
                solved[k * width : (k + 1) * width],
                preferred_element_type=jnp.float32,
            )
        reduced_out[i] = total.astype(jnp.bfloat16)

    from_cores(m_arrived)
    depth, m_width = m_blocks.shape[1:]
    share = n_row // n_col
    for i in range(n_tiles):
        total = jnp.zeros((rank, m_width), jnp.float32)
        for k in range(n_col):
            piece = m_blocks[k * share : (k + 1) * share]
            total += jnp.dot(
                cores_k[k, i],
                piece.reshape(share * depth, m_width),
                preferred_element_type=jnp.float32,
            )
        core_out[i] = total.astype(jnp.bfloat16)

    for copy in g_started + m_started + k_copies:
        copy.wait_send()


def update_kernel(
    core,
    reduced,
    bases_hbm,
    right_hbm,
    slab_hbm,
    rhs_hbm,
    slab_out_hbm,
    rhs_out_hbm,
    bases,
    right,
    slab,
    rhs,
    slab_out,
    rhs_out,
    load_sem,
    in_sem,
    out_sem,
):
    n_tiles, rank, wide = core.shape
    m_tiles = wide // rank
    order = bases.shape[0] // n_tiles
    chunks = [
        (pl.ds(i * order, order), pl.ds(j * order, order))
        for i in range(n_tiles)
        for j in range(m_tiles)
    ]
    first = [
        pltpu.make_async_copy(bases_hbm, bases, load_sem.at[0]),
        pltpu.make_async_copy(right_hbm, right, load_sem.at[1]),
    ]
    later = pltpu.make_async_copy(rhs_hbm, rhs, load_sem.at[2])
    loads = [
        pltpu.make_async_copy(slab_hbm.at[at], slab.at[at], in_sem.at[number])
        for number, at in enumerate(chunks)
    ]
    stores = [
        pltpu.make_async_copy(slab_out.at[at], slab_out_hbm.at[at], out_sem.at[number])
        for number, at in enumerate(chunks)
    ]
    for load in first + loads + [later]:
        load.start()
    for load in first:
        load.wait()
    for number, (at_row, at_col) in enumerate(chunks):
        i, j = number // m_tiles, number % m_tiles
        spread = jnp.dot(
            bases[at_row, :],
            core[i, :, j * rank : (j + 1) * rank],
            preferred_element_type=jnp.float32,
        ).astype(jnp.bfloat16)
        change = lax.dot_general(
            spread,
            right[at_col, :],
            (((1,), (1,)), ((), ())),
            preferred_element_type=jnp.float32,
        )
        loads[number].wait()
        slab_out[at_row, at_col] = (slab[at_row, at_col].astype(jnp.float32) - change).astype(
            jnp.bfloat16
        )
        stores[number].start()
    later.wait()
    for i in range(n_tiles):
        at = pl.ds(i * order, order)
        lowered = jnp.dot(bases[at, :], reduced[i], preferred_element_type=jnp.float32)
        rhs_out[at, :] = (rhs[at, :].astype(jnp.float32) - lowered).astype(jnp.bfloat16)
        store = pltpu.make_async_copy(
            rhs_out.at[at], rhs_out_hbm.at[at], out_sem.at[len(chunks) + i]
        )
        store.start()
        stores.append(store)
    for store in stores:
        store.wait()


def per_device(
    n_row,
    n_col,
    slab,
    panel_left,
    panel_top,
    row_bases,
    col_bases,
    row_ranks,
    col_ranks,
    pivot_inverse,
    pivot_rhs,
    rhs,
):
    order = pivot_inverse.shape[0]
    rank = row_bases.shape[1]
    n_tiles = row_ranks.shape[0]
    m_tiles = col_ranks.shape[0]
    gains = rhs.shape[1]
    width = panel_left.shape[1]
    outer, inner, cores = grid_of(n_row)
    sends = (outer - 1) + outer * (inner - 1) + outer * inner * (cores - 1)
    vmem = pl.BlockSpec(memory_space=pltpu.VMEM)
    hbm = pl.BlockSpec(memory_space=pltpu.HBM)
    core, reduced = pl.pallas_call(
        functools.partial(gather_kernel, n_row, n_col),
        out_shape=(
            jax.ShapeDtypeStruct((n_tiles, rank, m_tiles * rank), jnp.bfloat16),
            jax.ShapeDtypeStruct((n_tiles, rank, gains), jnp.bfloat16),
        ),
        in_specs=[hbm] * 8,
        out_specs=(vmem, vmem),
        scratch_shapes=[
            pltpu.SMEM(col_ranks.shape, col_ranks.dtype),
            pltpu.SMEM(row_ranks.shape, row_ranks.dtype),
            pltpu.VMEM(panel_top.shape, jnp.bfloat16),
            pltpu.VMEM(col_bases.shape, jnp.bfloat16),
            pltpu.VMEM(panel_left.shape, jnp.bfloat16),
            pltpu.VMEM(row_bases.shape, jnp.bfloat16),
            pltpu.VMEM(pivot_inverse.shape, jnp.bfloat16),
            pltpu.VMEM((n_row, panel_top.shape[0], m_tiles * rank), jnp.bfloat16),
            pltpu.VMEM((n_row, pivot_rhs.shape[0], gains), jnp.bfloat16),
            pltpu.VMEM((n_col, n_tiles, rank, width), jnp.bfloat16),
            pltpu.SemaphoreType.DMA((8,)),
            pltpu.SemaphoreType.DMA((sends,)),
            pltpu.SemaphoreType.DMA((n_row,)),
            pltpu.SemaphoreType.DMA((sends,)),
            pltpu.SemaphoreType.DMA((n_row,)),
            pltpu.SemaphoreType.DMA((max(n_col - 1, 1),)),
            pltpu.SemaphoreType.DMA((n_col,)),
        ],
        compiler_params=pltpu.CompilerParams(
            collective_id=0, has_side_effects=True, vmem_limit_bytes=62 * 2**20
        ),
        name="gather",
    )(col_ranks, row_ranks, panel_top, col_bases, panel_left, row_bases, pivot_inverse, pivot_rhs)

    return pl.pallas_call(
        update_kernel,
        out_shape=(
            jax.ShapeDtypeStruct(slab.shape, slab.dtype),
            jax.ShapeDtypeStruct(rhs.shape, rhs.dtype),
        ),
        in_specs=[vmem] * 2 + [hbm] * 4,
        out_specs=(hbm, hbm),
        scratch_shapes=[
            pltpu.VMEM(row_bases.shape, jnp.bfloat16),
            pltpu.VMEM(col_bases.shape, jnp.bfloat16),
            pltpu.VMEM(slab.shape, jnp.bfloat16),
            pltpu.VMEM(rhs.shape, jnp.bfloat16),
            pltpu.VMEM(slab.shape, jnp.bfloat16),
            pltpu.VMEM(rhs.shape, jnp.bfloat16),
            pltpu.SemaphoreType.DMA((3,)),
            pltpu.SemaphoreType.DMA((n_tiles * m_tiles,)),
            pltpu.SemaphoreType.DMA((n_tiles * m_tiles + n_tiles,)),
        ],
        compiler_params=pltpu.CompilerParams(vmem_limit_bytes=62 * 2**20),
        name="update",
    )(core, reduced, row_bases, col_bases, slab, rhs)


def solution(mesh):
    in_specs = (
        P("row", "col"),
        P("row", "col"),
        P("row", "col"),
        P("row", None),
        P("col", None),
        P("row"),
        P("col"),
        P(),
        P("row", "col"),
        P("row", "col"),
    )
    out_specs = (P("row", "col"), P("row", "col"))
    return jax.shard_map(
        functools.partial(per_device, mesh.shape["row"], mesh.shape["col"]),
        mesh=mesh,
        in_specs=in_specs,
        out_specs=out_specs,
        check_vma=False,
    )
```

time: 41.9 us -> 32.8 us (0.78)
  local copies, waits for them, and re-layouts: 13 us -> 0 us
  Pallas kernels: 27.7 us -> 32 us
    unnamed x24 -> x0, local copies, waits for them, and re-layouts: 13 us -> none
    pallas_call x1, Pallas kernels: 5.34 us -> 9.4 us  [per_device(): pl.pallas_call(update_kernel, out_shape=(jax.ShapeDtypeStruct(slab.shape,...]
where the time goes in v2:
time: 32.8 us; the launch traced here: 32.6 us
  Pallas kernels  32 us (98%)
  between operations  0.64 us (2%)
    pallas_call x1, Pallas kernels, per_device(): pl.pallas_call(functools.partial(gather_kernel, n_row, n_col), out_shape=...  22.6 us
    pallas_call x1, Pallas kernels, per_device(): pl.pallas_call(update_kernel, out_shape=(jax.ShapeDtypeStruct(slab.shape,...  9.4 us

profile of v2, /device:TPU:1, one launch (start us, length us, event | category | flops | bytes accessed | tf_op | source)
XLA Modules:
  0.0 32.6 jit_solution(5506150340632582634)
XLA Ops:
  0.6 22.6 %gather.1 = (bf16[2,256,1024]{2,1,0:T(8,128)(2,1)}, bf16[2,256,512]{2,1,0:T(8,128)(2,1)}) custom-call(s32[4]{0:T(128)} %col_ranks_hbm.1, s32[2]{0:T(128)} %row_ranks_hbm.1, bf16[32,2048]{1,0:T(8,128)(2,1)} %top_hbm.1, bf16[2048,256]{1,0:T(8,128)(2,1)} %right_hbm.3, bf16[1024,256]{1,0:T(8,128)(2,1)} %left_hbm.1, bf16[1024,256]{1,0:T(8,128)(2,1)} %bases_hbm.3, ...), custom_call_target="tpu_custom_call" | custom-call | tf_op jit(solution)/shard_map/gather/pallas_call | solution.py:339
  23.2 9.4 %update.1 = (bf16[1024,2048]{1,0:T(8,128)(2,1)}, bf16[1024,512]{1,0:T(8,128)(2,1)}) custom-call(bf16[2,256,1024]{2,1,0:T(8,128)(2,1)} %get-tuple-element.4.core, bf16[2,256,512]{2,1,0:T(8,128)(2,1)} %get-tuple-element.5.reduced, bf16[1024,256]{1,0:T(8,128)(2,1)} %bases_hbm.3, bf16[2048,256]{1,0:T(8,128)(2,1)} %right_hbm.3, bf16[1024,2048]{1,0:T(8,128)(2,1)} %slab_hbm.1, ...), custom_call_target="tpu_custom_call" | custom-call | tf_op jit(solution)/shard_map/update/pallas_call | solution.py:372

commit v3 on v2

--- a/solution.py
+++ b/solution.py
@@ -94,10 +94,18 @@
     for load in loads:
         load.start()
 
+    steps = [(k, way) for k in range(1, outer) for way in (1, -1)]
+
+    def inside(p):
+        return jnp.logical_and(p >= 0, p < outer)
+
+    def always(action):
+        action()
+
     def sender(blocks, send_sems, recv_sems):
         started = []
 
-        def send(which, target):
+        def send(which, target, when):
             copy = pltpu.make_async_remote_copy(
                 src_ref=blocks.at[which],
                 dst_ref=blocks.at[which],
@@ -106,11 +114,13 @@
                 device_id=(target, col),
                 device_id_type=MESH,
             )
-            copy.start()
-            started.append(copy)
-
-        def arrived(which):
-            pltpu.make_async_copy(blocks.at[which], blocks.at[which], recv_sems.at[which]).wait()
+            when(copy.start)
+            started.append((copy, when))
+
+        def arrived(which, when):
+            when(
+                pltpu.make_async_copy(blocks.at[which], blocks.at[which], recv_sems.at[which]).wait
+            )
 
         return started, send, arrived
 
@@ -118,33 +128,41 @@
     m_started, m_move, m_arrived = sender(m_blocks, m_send, m_recv)
 
     def send_own(move):
-        for p in reversed(a_peers):
-            move(row, index(p, b, c))
+        for way in (1, -1):
+            move(row, index(a + way, b, c), pl.when(inside(a + way)))
         for p in b_peers:
-            move(row, index(a, p, c))
+            move(row, index(a, p, c), always)
         for p in c_peers:
-            move(row, index(a, b, p))
-
-    def from_outer(p, move, landed):
-        s = index(p, b, c)
-        landed(s)
+            move(row, index(a, b, p), always)
+
+    def from_outer(k, way, move, landed):
+        when = pl.when(inside(a - way * k))
+        s = index(a - way * k, b, c)
+        landed(s, when)
+        if k < outer - 1:
+            move(
+                s,
+                index(a + way, b, c),
+                pl.when(jnp.logical_and(inside(a - way * k), inside(a + way))),
+            )
         for q in b_peers:
-            move(s, index(a, q, c))
+            move(s, index(a, q, c), when)
         for q in c_peers:
-            move(s, index(a, b, q))
-
-    def from_inner(a_, move, landed):
+            move(s, index(a, b, q), when)
+
+    def from_inner(k, way, move, landed):
+        when = pl.when(inside(a - way * k)) if k else always
         for p in b_peers:
-            s = index(a_, p, c)
-            landed(s)
+            s = index(a - way * k, p, c)
+            landed(s, when)
             for q in c_peers:
-                move(s, index(a, b, q))
+                move(s, index(a, b, q), when)
 
     def from_cores(landed):
         for q in c_peers:
-            for p in [a] + a_peers:
-                for r in [b] + b_peers:
-                    landed(index(p, r, q))
+            for p in range(outer):
+                for r in range(inner):
+                    landed(index(p, r, q), always)
 
     loads[0].wait()
     pl.semaphore_wait(barrier, len(partners))
@@ -163,8 +181,8 @@
         m_blocks[row, :, j * rank : (j + 1) * rank] = part.astype(jnp.bfloat16)
     send_own(m_move)
 
-    for p in a_peers:
-        from_outer(p, g_move, g_arrived)
+    for k, way in steps[:2]:
+        from_outer(k, way, g_move, g_arrived)
 
     for load in loads[5:]:
         load.wait()
@@ -191,14 +209,21 @@
         copy.start()
         k_copies.append(copy)
 
-    previous = a
-    for p in a_peers:
-        from_inner(previous, g_move, g_arrived)
-        from_outer(p, m_move, m_arrived)
-        from_inner(previous, m_move, m_arrived)
-        previous = p
-    from_inner(previous, g_move, g_arrived)
-    from_inner(previous, m_move, m_arrived)
+    from_inner(0, 1, g_move, g_arrived)
+    for k, way in steps[2:4]:
+        from_outer(k, way, g_move, g_arrived)
+    for k, way in steps[:2]:
+        from_outer(k, way, m_move, m_arrived)
+        from_inner(k, way, g_move, g_arrived)
+    from_inner(0, 1, m_move, m_arrived)
+    for k, way in steps[4:]:
+        from_outer(k, way, g_move, g_arrived)
+    for number, (k, way) in enumerate(steps[2:]):
+        from_outer(k, way, m_move, m_arrived)
+        from_inner(k, way, g_move, g_arrived)
+        from_inner(*steps[number], m_move, m_arrived)
+    for k, way in steps[-2:]:
+        from_inner(k, way, m_move, m_arrived)
 
     from_cores(g_arrived)
     solved = jnp.dot(
@@ -232,19 +257,23 @@
             )
         core_out[i] = total.astype(jnp.bfloat16)
 
-    for copy in g_started + m_started + k_copies:
+    for copy, when in g_started + m_started:
+        when(copy.wait_send)
+    for copy in k_copies:
         copy.wait_send()
 
 
 def update_kernel(
-    core,
-    reduced,
+    core_hbm,
+    reduced_hbm,
     bases_hbm,
     right_hbm,
     slab_hbm,
     rhs_hbm,
     slab_out_hbm,
     rhs_out_hbm,
+    core,
+    reduced,
     bases,
     right,
     slab,
@@ -264,10 +293,14 @@
         for j in range(m_tiles)
     ]
     first = [
+        pltpu.make_async_copy(core_hbm, core, load_sem.at[3]),
         pltpu.make_async_copy(bases_hbm, bases, load_sem.at[0]),
         pltpu.make_async_copy(right_hbm, right, load_sem.at[1]),
     ]
-    later = pltpu.make_async_copy(rhs_hbm, rhs, load_sem.at[2])
+    later = [
+        pltpu.make_async_copy(rhs_hbm, rhs, load_sem.at[2]),
+        pltpu.make_async_copy(reduced_hbm, reduced, load_sem.at[4]),
+    ]
     loads = [
         pltpu.make_async_copy(slab_hbm.at[at], slab.at[at], in_sem.at[number])
         for number, at in enumerate(chunks)
@@ -276,7 +309,7 @@
         pltpu.make_async_copy(slab_out.at[at], slab_out_hbm.at[at], out_sem.at[number])
         for number, at in enumerate(chunks)
     ]
-    for load in first + loads + [later]:
+    for load in first + loads + later:
         load.start()
     for load in first:
         load.wait()
@@ -298,7 +331,8 @@
             jnp.bfloat16
         )
         stores[number].start()
-    later.wait()
+    for load in later:
+        load.wait()
     for i in range(n_tiles):
         at = pl.ds(i * order, order)
         lowered = jnp.dot(bases[at, :], reduced[i], preferred_element_type=jnp.float32)
@@ -333,7 +367,8 @@
     gains = rhs.shape[1]
     width = panel_left.shape[1]
     outer, inner, cores = grid_of(n_row)
-    sends = (outer - 1) + outer * (inner - 1) + outer * inner * (cores - 1)
+    slots = 2 * outer - 1
+    sends = 2 * (outer - 1) + slots * (inner - 1) + slots * inner * (cores - 1)
     vmem = pl.BlockSpec(memory_space=pltpu.VMEM)
     hbm = pl.BlockSpec(memory_space=pltpu.HBM)
     core, reduced = pl.pallas_call(
@@ -375,16 +410,18 @@
             jax.ShapeDtypeStruct(slab.shape, slab.dtype),
             jax.ShapeDtypeStruct(rhs.shape, rhs.dtype),
         ),
-        in_specs=[vmem] * 2 + [hbm] * 4,
+        in_specs=[hbm] * 6,
         out_specs=(hbm, hbm),
         scratch_shapes=[
+            pltpu.VMEM(core.shape, jnp.bfloat16),
+            pltpu.VMEM(reduced.shape, jnp.bfloat16),
             pltpu.VMEM(row_bases.shape, jnp.bfloat16),
             pltpu.VMEM(col_bases.shape, jnp.bfloat16),
             pltpu.VMEM(slab.shape, jnp.bfloat16),
             pltpu.VMEM(rhs.shape, jnp.bfloat16),
             pltpu.VMEM(slab.shape, jnp.bfloat16),
             pltpu.VMEM(rhs.shape, jnp.bfloat16),
-            pltpu.SemaphoreType.DMA((3,)),
+            pltpu.SemaphoreType.DMA((5,)),
             pltpu.SemaphoreType.DMA((n_tiles * m_tiles,)),
             pltpu.SemaphoreType.DMA((n_tiles * m_tiles + n_tiles,)),
         ],

time: 32.8 us -> 34.1 us (1.040)
  Pallas kernels: 32 us -> 33.2 us
    pallas_call x1, Pallas kernels: 22.6 us -> 25 us  [per_device(): pl.pallas_call(functools.partial(gather_kernel, n_row, n_col), out_shape=...]
    pallas_call x1, Pallas kernels: 9.4 us -> 8.22 us  [per_device(): pl.pallas_call(update_kernel, out_shape=(jax.ShapeDtypeStruct(slab.shape,...]
where the time goes in v3:
time: 34.1 us; the launch traced here: 33.9 us
  Pallas kernels  33.2 us (97%)
  between operations  0.64 us (2%)
    pallas_call x1, Pallas kernels, per_device(): pl.pallas_call(functools.partial(gather_kernel, n_row, n_col), out_shape=...  25 us
    pallas_call x1, Pallas kernels, per_device(): pl.pallas_call(update_kernel, out_shape=(jax.ShapeDtypeStruct(slab.shape,...  8.22 us

profile of v3, /device:TPU:1, one launch (start us, length us, event | category | flops | bytes accessed | tf_op | source)
XLA Modules:
  0.0 33.9 jit_solution(8094644320406947531)
XLA Ops:
  0.6 25.0 %gather.1 = (bf16[2,256,1024]{2,1,0:T(8,128)(2,1)}, bf16[2,256,512]{2,1,0:T(8,128)(2,1)}) custom-call(s32[4]{0:T(128)} %col_ranks_hbm.1, s32[2]{0:T(128)} %row_ranks_hbm.1, bf16[32,2048]{1,0:T(8,128)(2,1)} %top_hbm.1, bf16[2048,256]{1,0:T(8,128)(2,1)} %right_hbm.3, bf16[1024,256]{1,0:T(8,128)(2,1)} %left_hbm.1, bf16[1024,256]{1,0:T(8,128)(2,1)} %bases_hbm.3, ...), custom_call_target="tpu_custom_call" | custom-call | tf_op jit(solution)/shard_map/gather/pallas_call | solution.py:374
  25.6 8.2 %update.1 = (bf16[1024,2048]{1,0:T(8,128)(2,1)}, bf16[1024,512]{1,0:T(8,128)(2,1)}) custom-call(bf16[2,256,1024]{2,1,0:T(8,128)(2,1)} %get-tuple-element.4.core_hbm, bf16[2,256,512]{2,1,0:T(8,128)(2,1)} %get-tuple-element.5.reduced_hbm, bf16[1024,256]{1,0:T(8,128)(2,1)} %bases_hbm.3, bf16[2048,256]{1,0:T(8,128)(2,1)} %right_hbm.3, ...), custom_call_target="tpu_custom_call" | custom-call | tf_op jit(solution)/shard_map/update/pallas_call | solution.py:407

commit v4 on v3

--- a/solution.py
+++ b/solution.py
@@ -128,8 +128,8 @@
     m_started, m_move, m_arrived = sender(m_blocks, m_send, m_recv)
 
     def send_own(move):
-        for way in (1, -1):
-            move(row, index(a + way, b, c), pl.when(inside(a + way)))
+        for k, way in steps:
+            move(row, index(a + way * k, b, c), pl.when(inside(a + way * k)))
         for p in b_peers:
             move(row, index(a, p, c), always)
         for p in c_peers:
@@ -139,12 +139,6 @@
         when = pl.when(inside(a - way * k))
         s = index(a - way * k, b, c)
         landed(s, when)
-        if k < outer - 1:
-            move(
-                s,
-                index(a + way, b, c),
-                pl.when(jnp.logical_and(inside(a - way * k), inside(a + way))),
-            )
         for q in b_peers:
             move(s, index(a, q, c), when)
         for q in c_peers:

time: 34.1 us -> 31.7 us (0.930)
  Pallas kernels: 33.2 us -> 30.8 us
    pallas_call x1, Pallas kernels: 25 us -> 22.6 us  [per_device(): pl.pallas_call(functools.partial(gather_kernel, n_row, n_col), out_shape=...]
where the time goes in v4:
time: 31.7 us; the launch traced here: 31.4 us
  Pallas kernels  30.8 us (97%)
  between operations  0.64 us (2%)
    pallas_call x1, Pallas kernels, per_device(): pl.pallas_call(functools.partial(gather_kernel, n_row, n_col), out_shape=...  22.6 us
    pallas_call x1, Pallas kernels, per_device(): pl.pallas_call(update_kernel, out_shape=(jax.ShapeDtypeStruct(slab.shape,...  8.22 us

profile of v4, /device:TPU:1, one launch (start us, length us, event | category | flops | bytes accessed | tf_op | source)
XLA Modules:
  0.0 31.4 jit_solution(1669994242666786154)
XLA Ops:
  0.6 22.6 %gather.1 = (bf16[2,256,1024]{2,1,0:T(8,128)(2,1)}, bf16[2,256,512]{2,1,0:T(8,128)(2,1)}) custom-call(s32[4]{0:T(128)} %col_ranks_hbm.1, s32[2]{0:T(128)} %row_ranks_hbm.1, bf16[32,2048]{1,0:T(8,128)(2,1)} %top_hbm.1, bf16[2048,256]{1,0:T(8,128)(2,1)} %right_hbm.3, bf16[1024,256]{1,0:T(8,128)(2,1)} %left_hbm.1, bf16[1024,256]{1,0:T(8,128)(2,1)} %bases_hbm.3, ...), custom_call_target="tpu_custom_call" | custom-call | tf_op jit(solution)/shard_map/gather/pallas_call | solution.py:368
  23.2 8.2 %update.1 = (bf16[1024,2048]{1,0:T(8,128)(2,1)}, bf16[1024,512]{1,0:T(8,128)(2,1)}) custom-call(bf16[2,256,1024]{2,1,0:T(8,128)(2,1)} %get-tuple-element.4.core_hbm, bf16[2,256,512]{2,1,0:T(8,128)(2,1)} %get-tuple-element.5.reduced_hbm, bf16[1024,256]{1,0:T(8,128)(2,1)} %bases_hbm.3, bf16[2048,256]{1,0:T(8,128)(2,1)} %right_hbm.3, ...), custom_call_target="tpu_custom_call" | custom-call | tf_op jit(solution)/shard_map/update/pallas_call | solution.py:401

commit v5 on v4

--- a/solution.py
+++ b/solution.py
@@ -28,6 +28,8 @@
     bases_hbm,
     inverse_hbm,
     pivot_hbm,
+    core_hbm,
+    reduced_hbm,
     core_out,
     reduced_out,
     col_ranks,
@@ -41,6 +43,7 @@
     g_blocks,
     cores_k,
     load_sem,
+    store_sem,
     m_send,
     m_recv,
     g_send,
@@ -237,6 +240,9 @@
             )
         reduced_out[i] = total.astype(jnp.bfloat16)
 
+    stores = [pltpu.make_async_copy(reduced_out, reduced_hbm, store_sem.at[n_tiles])]
+    stores[0].start()
+
     from_cores(m_arrived)
     depth, m_width = m_blocks.shape[1:]
     share = n_row // n_col
@@ -250,11 +256,16 @@
                 preferred_element_type=jnp.float32,
             )
         core_out[i] = total.astype(jnp.bfloat16)
+        store = pltpu.make_async_copy(core_out.at[i], core_hbm.at[i], store_sem.at[i])
+        store.start()
+        stores.append(store)
 
     for copy, when in g_started + m_started:
         when(copy.wait_send)
     for copy in k_copies:
         copy.wait_send()
+    for store in stores:
+        store.wait()
 
 
 def update_kernel(
@@ -363,7 +374,6 @@
     outer, inner, cores = grid_of(n_row)
     slots = 2 * outer - 1
     sends = 2 * (outer - 1) + slots * (inner - 1) + slots * inner * (cores - 1)
-    vmem = pl.BlockSpec(memory_space=pltpu.VMEM)
     hbm = pl.BlockSpec(memory_space=pltpu.HBM)
     core, reduced = pl.pallas_call(
         functools.partial(gather_kernel, n_row, n_col),
@@ -372,8 +382,10 @@
             jax.ShapeDtypeStruct((n_tiles, rank, gains), jnp.bfloat16),
         ),
         in_specs=[hbm] * 8,
-        out_specs=(vmem, vmem),
+        out_specs=(hbm, hbm),
         scratch_shapes=[
+            pltpu.VMEM((n_tiles, rank, m_tiles * rank), jnp.bfloat16),
+            pltpu.VMEM((n_tiles, rank, gains), jnp.bfloat16),
             pltpu.SMEM(col_ranks.shape, col_ranks.dtype),
             pltpu.SMEM(row_ranks.shape, row_ranks.dtype),
             pltpu.VMEM(panel_top.shape, jnp.bfloat16),
@@ -385,6 +397,7 @@
             pltpu.VMEM((n_row, pivot_rhs.shape[0], gains), jnp.bfloat16),
             pltpu.VMEM((n_col, n_tiles, rank, width), jnp.bfloat16),
             pltpu.SemaphoreType.DMA((8,)),
+            pltpu.SemaphoreType.DMA((n_tiles + 1,)),
             pltpu.SemaphoreType.DMA((sends,)),
             pltpu.SemaphoreType.DMA((n_row,)),
             pltpu.SemaphoreType.DMA((sends,)),

time: 31.7 us -> 31.3 us (0.987)
  Pallas kernels: 30.8 us -> 30.4 us
    pallas_call x1, Pallas kernels: 22.6 us -> 22.2 us  [per_device(): pl.pallas_call(functools.partial(gather_kernel, n_row, n_col), out_shape=...]
where the time goes in v5:
time: 31.3 us; the launch traced here: 31.1 us
  Pallas kernels  30.4 us (97%)
  between operations  0.64 us (2%)
    pallas_call x1, Pallas kernels, per_device(): pl.pallas_call(functools.partial(gather_kernel, n_row, n_col), out_shape=...  22.2 us
    pallas_call x1, Pallas kernels, per_device(): pl.pallas_call(update_kernel, out_shape=(jax.ShapeDtypeStruct(slab.shape,...  8.22 us

profile of v5, /device:TPU:1, one launch (start us, length us, event | category | flops | bytes accessed | tf_op | source)
XLA Modules:
  0.0 31.1 jit_solution(6948567083578890192)
XLA Ops:
  0.6 22.2 %gather.1 = (bf16[2,256,1024]{2,1,0:T(8,128)(2,1)}, bf16[2,256,512]{2,1,0:T(8,128)(2,1)}) custom-call(s32[4]{0:T(128)} %col_ranks_hbm.1, s32[2]{0:T(128)} %row_ranks_hbm.1, bf16[32,2048]{1,0:T(8,128)(2,1)} %top_hbm.1, bf16[2048,256]{1,0:T(8,128)(2,1)} %right_hbm.3, bf16[1024,256]{1,0:T(8,128)(2,1)} %left_hbm.1, bf16[1024,256]{1,0:T(8,128)(2,1)} %bases_hbm.3, ...), custom_call_target="tpu_custom_call" | custom-call | tf_op jit(solution)/shard_map/gather/pallas_call | solution.py:378
  22.8 8.2 %update.1 = (bf16[1024,2048]{1,0:T(8,128)(2,1)}, bf16[1024,512]{1,0:T(8,128)(2,1)}) custom-call(bf16[2,256,1024]{2,1,0:T(8,128)(2,1)} %get-tuple-element.4.core_hbm, bf16[2,256,512]{2,1,0:T(8,128)(2,1)} %get-tuple-element.5.reduced_hbm, bf16[1024,256]{1,0:T(8,128)(2,1)} %bases_hbm.3, bf16[2048,256]{1,0:T(8,128)(2,1)} %right_hbm.3, ...), custom_call_target="tpu_custom_call" | custom-call | tf_op jit(solution)/shard_map/update/pallas_call | solution.py:414
